TPU v7x, 128 devices: a whole 4x4x4 slice. The times are simulated.
128 devices in a mesh: row: 4 (over z_hi, core), col: 16 (over y, x), layer: 2 (over z_lo).
Axes of the slice: x: 4, y: 4, z: 4 (z_hi: 2, z_lo: 2; z = z_hi * 2 + z_lo), core: 2. Of those that a mesh axis runs over, the one named last changes fastest.
Arguments:
- x_blocks: bfloat16 [6, 16, 3, 16, 128, 128], P(None, 'row', None, 'col'), may hold values from -0.375 to 0.375
- present: int32 [6, 16, 3, 16], P(None, 'row', None, 'col'), may hold values 0 or 1
Outputs:
- purified: float32 [4, 16, 3, 16, 128, 128], P('layer', 'row', None, 'col')
All inputs are finite; a program needn't handle non-finite values. No bound on the sum of `present` on one device may be relied on, other than what follows from the above.
Results may differ from a plain program's by a relative error of at most 0.0026.
Values may be sent and summed in bfloat16 or wider, within the bound.
A program may use at most 64 MiB of HBM per device.

v0:
```python
import jax
import jax.numpy as jnp
from jax import lax
from jax.sharding import PartitionSpec as P


def shifted_2(array, axis, by):
    length = lax.axis_size(axis)
    return lax.ppermute(array, axis, [(i, (i + by) % length) for i in range(length)])


def contract(left_blocks, right_blocks, region_count):
    columns_out = []
    for e_index in range(3):
        valid_offsets = [d_index for d_index in range(3) if 0 <= e_index - d_index + 1 <= 2]
        left_stack = jnp.stack([left_blocks[:, :, d_index] for d_index in valid_offsets], axis=2)
        right_stack = jnp.stack(
            [
                right_blocks[d_index : d_index + region_count, :, e_index - d_index + 1]
                for d_index in valid_offsets
            ],
            axis=1,
        )
        columns_out.append(
            jnp.einsum(
                "brdcxy,bdcwyz->brwxz", left_stack, right_stack, preferred_element_type=jnp.float32
            )
        )
    return jnp.stack(columns_out, axis=2)


def local(x_blocks, present):
    region_count = x_blocks.shape[0] - 2
    col_classes = x_blocks.shape[3]
    col_count = lax.axis_size("col")
    layer_count = lax.axis_size("layer")
    layer_steps = col_count // layer_count
    column = lax.axis_index("col")
    layer_index = lax.axis_index("layer")
    masked = x_blocks * present.astype(jnp.bfloat16)[..., None, None]
    kept_rows = present[1 : region_count + 1].astype(jnp.float32)[..., None, None]
    half_rows = region_count // layer_count
    panel_all = lax.all_gather(masked, "row", axis=1, tiled=True)

    def fetch_group(class_group):
        return lax.dynamic_slice_in_dim(panel_all, class_group * col_classes, col_classes, 1)

    def product(left_blocks):
        shifted = shifted_2(left_blocks, "col", -layer_steps)
        start_group = layer_index * layer_steps
        group_stride = 1
        moving = jnp.where(layer_index == 0, left_blocks, shifted)
        summed = jnp.zeros(left_blocks.shape, jnp.float32)

        def cannon_turn(turn_index, state_pair):
            moving_blocks, running = state_pair
            class_group = (column + start_group + group_stride * turn_index) % col_count
            running = running + contract(moving_blocks, fetch_group(class_group), region_count)
            moving_blocks = shifted_2(moving_blocks, "col", -1)
            return (moving_blocks, running)

        moving, summed = lax.fori_loop(0, layer_steps - 1, cannon_turn, (moving, summed))
        class_group = (column + start_group + group_stride * (layer_steps - 1)) % col_count
        return summed + contract(moving, fetch_group(class_group), region_count)

    square = lax.psum(product(masked[1 : region_count + 1]), "layer") * kept_rows
    cubed = lax.psum_scatter(
        product(square.astype(jnp.bfloat16)), "layer", scatter_dimension=0, tiled=True
    )
    square_half = lax.dynamic_slice_in_dim(square, layer_index * half_rows, half_rows, 0)
    kept_half = lax.dynamic_slice_in_dim(kept_rows, layer_index * half_rows, half_rows, 0)
    return 3.0 * square_half - 2.0 * cubed * kept_half


def solution(mesh):
    return jax.shard_map(
        local,
        mesh=mesh,
        in_specs=(P(None, "row", None, "col", None, None), P(None, "row", None, "col")),
        out_specs=P("layer", "row", None, "col", None, None),
        check_vma=False,
    )
```

profile of v0, /device:TPU:0, one launch (start us, length us, event | category | flops | bytes accessed | tf_op | source)
XLA Modules:
  0.0 851.4 jit_solution(3739690995629908041)
XLA Ops:
  6.5 3.1 copy.21
  9.8 1.6 broadcast_multiply_fusion.1
  11.5 1.6 copy-done.6
  14.3 3.3 collective-permute-start.2
  17.6 34.7 %collective-permute-done.2 = bf16[4,4,3,1,128,128]{4,5,1,0,3,2:T(8,128)(2,1)} collective-permute-done((bf16[4,4,3,1,128,128]{4,5,1,0,3,2:T(8,128)(2,1)}, bf16[4,4,3,1,128,128]{4,5,1,0,3,2:T(8,128)(2,1)}, u32[]{:S(2)}, u32[]{:S(2)}) %collective-permute-start.2) | collective-permute-done | bytes 1572896 | tf_op jit(solution)/shard_map/ppermute | solution.py:9
  52.3 1.3 broadcast_select_fusion.1
  53.6 1.9 copy.22
  55.5 26.9 %all-gather.2.cloned.1.call-done = bf16[6,16,3,1,128,128]{4,5,1,0,3,2:T(8,128)(2,1)} async-done(((bf16[6,4,3,1,128,128]{4,5,1,0,3,2:T(8,128)(2,1)}), bf16[6,16,3,1,128,128]{4,5,1,0,3,2:T(8,128)(2,1)}) %all-gather.2.cloned.1.call-update) | async-done | bytes 9437200 | tf_op jit(solution)/shard_map/all_gather | solution.py:43
  82.5 2.0 constant_dynamic-slice_fusion.19
  84.5 261.2 %while.36 = (s32[]{:T(128)}, bf16[4,4,3,1,128,128]{5,4,2,1,0,3:T(8,128)(2,1)S(1)}, f32[4,4,3,1,128,128]{4,5,1,0,3,2:T(8,128)}, s32[]{:T(128)}, bf16[6,16,3,1,128...) while((s32[]{:T(128)}, ...), condition=%wide.region_1.2_spmd.clone, body=%wide.region_0.1_spmd.clone.sunk | while | flops 475136000 | bytes 53608852 | solution.py:62
  84.7 4.9 collective-permute-start
  89.6 1.3 constant_dynamic-slice_fusion.23
  94.4 29.3 %collective-permute-done = bf16[4,4,3,1,128,128]{5,4,2,1,0,3:T(8,128)(2,1)S(1)} collective-permute-done((bf16[4,4,3,1,128,128]{5,4,2,1,0,3:T(8,128)(2,1)S(1)}, bf16[4,4,3,1,128,128]{5,4,2,1,0,3:T(8,128)(2,1)S(1)}, u32[]{:S(2)}, u32[]{:S(2)}) %collective-permute-start) | collective-permute-done | bytes 1572896 | tf_op jit(solution)/shard_map/while/body/eval_jaxpr/ppermute | solution.py:9
  123.9 5.9 collective-permute-start
  129.7 1.3 constant_dynamic-slice_fusion.23
  134.5 28.5 %collective-permute-done = bf16[4,4,3,1,128,128]{5,4,2,1,0,3:T(8,128)(2,1)S(1)} collective-permute-done((bf16[4,4,3,1,128,128]{5,4,2,1,0,3:T(8,128)(2,1)S(1)}, bf16[4,4,3,1,128,128]{5,4,2,1,0,3:T(8,128)(2,1)S(1)}, u32[]{:S(2)}, u32[]{:S(2)}) %collective-permute-start) | collective-permute-done | bytes 1572896 | tf_op jit(solution)/shard_map/while/body/eval_jaxpr/ppermute | solution.py:9
  163.2 5.9 collective-permute-start
  169.1 1.3 constant_dynamic-slice_fusion.23
  173.9 27.5 %collective-permute-done = bf16[4,4,3,1,128,128]{5,4,2,1,0,3:T(8,128)(2,1)S(1)} collective-permute-done((bf16[4,4,3,1,128,128]{5,4,2,1,0,3:T(8,128)(2,1)S(1)}, bf16[4,4,3,1,128,128]{5,4,2,1,0,3:T(8,128)(2,1)S(1)}, u32[]{:S(2)}, u32[]{:S(2)}) %collective-permute-start) | collective-permute-done | bytes 1572896 | tf_op jit(solution)/shard_map/while/body/eval_jaxpr/ppermute | solution.py:9
  201.6 5.9 collective-permute-start
  207.4 1.3 constant_dynamic-slice_fusion.23
  212.2 26.6 %collective-permute-done = bf16[4,4,3,1,128,128]{5,4,2,1,0,3:T(8,128)(2,1)S(1)} collective-permute-done((bf16[4,4,3,1,128,128]{5,4,2,1,0,3:T(8,128)(2,1)S(1)}, bf16[4,4,3,1,128,128]{5,4,2,1,0,3:T(8,128)(2,1)S(1)}, u32[]{:S(2)}, u32[]{:S(2)}) %collective-permute-start) | collective-permute-done | bytes 1572896 | tf_op jit(solution)/shard_map/while/body/eval_jaxpr/ppermute | solution.py:9
  239.0 5.9 collective-permute-start
  244.9 1.3 constant_dynamic-slice_fusion.23
  249.7 25.7 %collective-permute-done = bf16[4,4,3,1,128,128]{5,4,2,1,0,3:T(8,128)(2,1)S(1)} collective-permute-done((bf16[4,4,3,1,128,128]{5,4,2,1,0,3:T(8,128)(2,1)S(1)}, bf16[4,4,3,1,128,128]{5,4,2,1,0,3:T(8,128)(2,1)S(1)}, u32[]{:S(2)}, u32[]{:S(2)}) %collective-permute-start) | collective-permute-done | bytes 1572896 | tf_op jit(solution)/shard_map/while/body/eval_jaxpr/ppermute | solution.py:9
  275.6 5.9 collective-permute-start
  281.5 1.3 constant_dynamic-slice_fusion.23
  286.3 24.8 %collective-permute-done = bf16[4,4,3,1,128,128]{5,4,2,1,0,3:T(8,128)(2,1)S(1)} collective-permute-done((bf16[4,4,3,1,128,128]{5,4,2,1,0,3:T(8,128)(2,1)S(1)}, bf16[4,4,3,1,128,128]{5,4,2,1,0,3:T(8,128)(2,1)S(1)}, u32[]{:S(2)}, u32[]{:S(2)}) %collective-permute-start) | collective-permute-done | bytes 1572896 | tf_op jit(solution)/shard_map/while/body/eval_jaxpr/ppermute | solution.py:9
  311.2 5.9 collective-permute-start
  317.1 1.3 constant_dynamic-slice_fusion.23
  321.9 23.9 %collective-permute-done = bf16[4,4,3,1,128,128]{5,4,2,1,0,3:T(8,128)(2,1)S(1)} collective-permute-done((bf16[4,4,3,1,128,128]{5,4,2,1,0,3:T(8,128)(2,1)S(1)}, bf16[4,4,3,1,128,128]{5,4,2,1,0,3:T(8,128)(2,1)S(1)}, u32[]{:S(2)}, u32[]{:S(2)}) %collective-permute-start) | collective-permute-done | bytes 1572896 | tf_op jit(solution)/shard_map/while/body/eval_jaxpr/ppermute | solution.py:9
  345.7 1.5 convolution_bitcast_fusion.7
  349.1 2.4 maximum_add_fusion.2
  351.8 92.0 %all-reduce.4.cloned.1.call-done = f32[4,4,3,1,128,128]{4,5,1,0,3,2:T(8,128)} async-done(((f32[4,4,3,1,128,128]{4,5,1,0,3,2:T(8,128)}), f32[4,4,3,1,128,128]{4,5,1,0,3,2:T(8,128)}) %all-reduce.4.cloned.1.call-update) | async-done | bytes 3145744 | tf_op jit(solution)/shard_map/psum | solution.py:66
  443.7 4.0 fusion.65
  447.8 3.0 collective-permute-start.3
  450.8 34.7 %collective-permute-done.3 = bf16[4,4,3,1,128,128]{4,5,1,0,3,2:T(8,128)(2,1)} collective-permute-done((bf16[4,4,3,1,128,128]{4,5,1,0,3,2:T(8,128)(2,1)S(1)}, bf16[4,4,3,1,128,128]{4,5,1,0,3,2:T(8,128)(2,1)}, u32[]{:S(2)}, u32[]{:S(2)}) %collective-permute-start.3) | collective-permute-done | bytes 1572896 | tf_op jit(solution)/shard_map/ppermute | solution.py:9
  486.6 251.9 %while.37 = (s32[]{:T(128)}, bf16[4,4,3,1,128,128]{5,4,2,1,0,3:T(8,128)(2,1)S(1)}, f32[4,4,3,1,128,128]{4,5,1,0,3,2:T(8,128)}, s32[]{:T(128)}, bf16[6,16,3,1,128...) while((s32[]{:T(128)}, ...), condition=%wide.region_4.5_spmd.clone, body=%wide.region_3.4_spmd.clone.sunk | while | flops 475136000 | bytes 53608852 | solution.py:62
  486.8 4.9 collective-permute-start.1
  491.7 1.3 constant_dynamic-slice_fusion.24
  496.5 28.0 %collective-permute-done.1 = bf16[4,4,3,1,128,128]{5,4,2,1,0,3:T(8,128)(2,1)S(1)} collective-permute-done((bf16[4,4,3,1,128,128]{5,4,2,1,0,3:T(8,128)(2,1)S(1)}, bf16[4,4,3,1,128,128]{5,4,2,1,0,3:T(8,128)(2,1)S(1)}, u32[]{:S(2)}, u32[]{:S(2)}) %collective-permute-start.1) | collective-permute-done | bytes 1572896 | tf_op jit(solution)/shard_map/while/body/eval_jaxpr/ppermute | solution.py:9
  524.7 5.9 collective-permute-start.1
  530.5 1.3 constant_dynamic-slice_fusion.24
  535.3 27.1 %collective-permute-done.1 = bf16[4,4,3,1,128,128]{5,4,2,1,0,3:T(8,128)(2,1)S(1)} collective-permute-done((bf16[4,4,3,1,128,128]{5,4,2,1,0,3:T(8,128)(2,1)S(1)}, bf16[4,4,3,1,128,128]{5,4,2,1,0,3:T(8,128)(2,1)S(1)}, u32[]{:S(2)}, u32[]{:S(2)}) %collective-permute-start.1) | collective-permute-done | bytes 1572896 | tf_op jit(solution)/shard_map/while/body/eval_jaxpr/ppermute | solution.py:9
  562.6 5.9 collective-permute-start.1
  568.4 1.3 constant_dynamic-slice_fusion.24
  573.2 26.1 %collective-permute-done.1 = bf16[4,4,3,1,128,128]{5,4,2,1,0,3:T(8,128)(2,1)S(1)} collective-permute-done((bf16[4,4,3,1,128,128]{5,4,2,1,0,3:T(8,128)(2,1)S(1)}, bf16[4,4,3,1,128,128]{5,4,2,1,0,3:T(8,128)(2,1)S(1)}, u32[]{:S(2)}, u32[]{:S(2)}) %collective-permute-start.1) | collective-permute-done | bytes 1572896 | tf_op jit(solution)/shard_map/while/body/eval_jaxpr/ppermute | solution.py:9
  599.6 5.9 collective-permute-start.1
  605.4 1.3 constant_dynamic-slice_fusion.24
  610.2 25.2 %collective-permute-done.1 = bf16[4,4,3,1,128,128]{5,4,2,1,0,3:T(8,128)(2,1)S(1)} collective-permute-done((bf16[4,4,3,1,128,128]{5,4,2,1,0,3:T(8,128)(2,1)S(1)}, bf16[4,4,3,1,128,128]{5,4,2,1,0,3:T(8,128)(2,1)S(1)}, u32[]{:S(2)}, u32[]{:S(2)}) %collective-permute-start.1) | collective-permute-done | bytes 1572896 | tf_op jit(solution)/shard_map/while/body/eval_jaxpr/ppermute | solution.py:9
  635.6 5.9 collective-permute-start.1
  641.5 1.3 constant_dynamic-slice_fusion.24
  646.3 24.3 %collective-permute-done.1 = bf16[4,4,3,1,128,128]{5,4,2,1,0,3:T(8,128)(2,1)S(1)} collective-permute-done((bf16[4,4,3,1,128,128]{5,4,2,1,0,3:T(8,128)(2,1)S(1)}, bf16[4,4,3,1,128,128]{5,4,2,1,0,3:T(8,128)(2,1)S(1)}, u32[]{:S(2)}, u32[]{:S(2)}) %collective-permute-start.1) | collective-permute-done | bytes 1572896 | tf_op jit(solution)/shard_map/while/body/eval_jaxpr/ppermute | solution.py:9
  670.8 5.9 collective-permute-start.1
  676.6 1.3 constant_dynamic-slice_fusion.24
  681.4 23.7 %collective-permute-done.1 = bf16[4,4,3,1,128,128]{5,4,2,1,0,3:T(8,128)(2,1)S(1)} collective-permute-done((bf16[4,4,3,1,128,128]{5,4,2,1,0,3:T(8,128)(2,1)S(1)}, bf16[4,4,3,1,128,128]{5,4,2,1,0,3:T(8,128)(2,1)S(1)}, u32[]{:S(2)}, u32[]{:S(2)}) %collective-permute-start.1) | collective-permute-done | bytes 1572896 | tf_op jit(solution)/shard_map/while/body/eval_jaxpr/ppermute | solution.py:9
  705.3 5.9 collective-permute-start.1
  711.2 1.3 constant_dynamic-slice_fusion.24
  716.0 22.5 %collective-permute-done.1 = bf16[4,4,3,1,128,128]{5,4,2,1,0,3:T(8,128)(2,1)S(1)} collective-permute-done((bf16[4,4,3,1,128,128]{5,4,2,1,0,3:T(8,128)(2,1)S(1)}, bf16[4,4,3,1,128,128]{5,4,2,1,0,3:T(8,128)(2,1)S(1)}, u32[]{:S(2)}, u32[]{:S(2)}) %collective-permute-start.1) | collective-permute-done | bytes 1572896 | tf_op jit(solution)/shard_map/while/body/eval_jaxpr/ppermute | solution.py:9
  738.5 1.5 convolution_bitcast_fusion.5
  741.9 2.4 maximum_add_fusion.3
  746.2 92.9 %all-reduce.6.cloned.1.call-done = f32[4,4,3,1,128,128]{4,5,1,0,3,2:T(8,128)} async-done(((f32[4,4,3,1,128,128]{4,5,1,0,3,2:T(8,128)}), f32[4,4,3,1,128,128]{4,5,1,0,3,2:T(8,128)}) %all-reduce.6.cloned.1.call-update) | async-done | bytes 3145744
  839.0 2.8 fusion.40
  841.8 3.0 copy.27
  (170 shorter events, 58.2 us)
Async XLA Ops:
  6.5 3.1 copy-start.12
  6.5 75.9 %all-gather.2.cloned.1.call-start = ((), (), s32[]{:S(2)}) async-start(), calls=%async_computation | async-start | bytes 11796480 | tf_op jit(solution)/shard_map/all_gather | solution.py:43
  11.4 1.7 copy-start.6
  11.4 432.3 %all-reduce.4.cloned.1.call-start = ((), (), s32[]{:S(2)}) async-start(), calls=%async_computation.1 | async-start | bytes 6291456 | tf_op jit(solution)/shard_map/psum | solution.py:66
  14.3 38.0 %collective-permute-start.2 = (bf16[4,4,3,1,128,128]{4,5,1,0,3,2:T(8,128)(2,1)}, bf16[4,4,3,1,128,128]{4,5,1,0,3,2:T(8,128)(2,1)}, u32[]{:S(2)}, u32[]{:S(2)}) collective-permute-start(bf16[4,4,3,1,128,128]{4,5,1,0,3,2:T(8,128)(2,1)} %slice.269), channel_id=1, source_target_pairs={{0,16},{2,18},{4,20},{6,22},{8,24},{10,26},{12,28},{14,30},{16,0},... | collective-permute-start | bytes 4718600 | tf_op jit(solution)/shard_map/ppermute | solution.py:9
  84.7 39.0 %collective-permute-start = (bf16[4,4,3,1,128,128]{5,4,2,1,0,3:T(8,128)(2,1)S(1)}, bf16[4,4,3,1,128,128]{5,4,2,1,0,3:T(8,128)(2,1)S(1)}, u32[]{:S(2)}, u32[]{:S(2)}) collective-permute-start(bf16[4,4,3,1,128,128]{5,4,2,1,0,3:T(8,128)(2,1)S(1)} %copy.62), channel_id=1, source_target_pairs={{0,30},{2,0},{4,2},{6,4},{8,6},{10,8},{12,10},{14,12},{16,14},{18,... | collective-permute-start | bytes 4718600 | tf_op jit(solution)/shard_map/while/body/eval_jaxpr/ppermute | solution.py:9
  91.4 1.9 copy-start
  94.4 29.3 %copy-start.1 = (f32[4,4,3,1,128,128]{4,5,1,0,3,2:T(8,128)}, f32[4,4,3,1,128,128]{4,5,1,0,3,2:T(8,128)S(1)}, u32[]{:S(2)}) copy-start(f32[4,4,3,1,128,128]{4,5,1,0,3,2:T(8,128)S(1)} %maximum_add_fusion.6) | copy-start | bytes 9437188 | tf_op jit(solution)/shard_map/while
  123.9 39.1 %collective-permute-start = (bf16[4,4,3,1,128,128]{5,4,2,1,0,3:T(8,128)(2,1)S(1)}, bf16[4,4,3,1,128,128]{5,4,2,1,0,3:T(8,128)(2,1)S(1)}, u32[]{:S(2)}, u32[]{:S(2)}) collective-permute-start(bf16[4,4,3,1,128,128]{5,4,2,1,0,3:T(8,128)(2,1)S(1)} %copy.62), channel_id=1, source_target_pairs={{0,30},{2,0},{4,2},{6,4},{8,6},{10,8},{12,10},{14,12},{16,14},{18,... | collective-permute-start | bytes 4718600 | tf_op jit(solution)/shard_map/while/body/eval_jaxpr/ppermute | solution.py:9
  131.6 1.9 copy-start
  134.5 28.5 %copy-start.1 = (f32[4,4,3,1,128,128]{4,5,1,0,3,2:T(8,128)}, f32[4,4,3,1,128,128]{4,5,1,0,3,2:T(8,128)S(1)}, u32[]{:S(2)}) copy-start(f32[4,4,3,1,128,128]{4,5,1,0,3,2:T(8,128)S(1)} %maximum_add_fusion.6) | copy-start | bytes 9437188 | tf_op jit(solution)/shard_map/while
  163.2 38.2 %collective-permute-start = (bf16[4,4,3,1,128,128]{5,4,2,1,0,3:T(8,128)(2,1)S(1)}, bf16[4,4,3,1,128,128]{5,4,2,1,0,3:T(8,128)(2,1)S(1)}, u32[]{:S(2)}, u32[]{:S(2)}) collective-permute-start(bf16[4,4,3,1,128,128]{5,4,2,1,0,3:T(8,128)(2,1)S(1)} %copy.62), channel_id=1, source_target_pairs={{0,30},{2,0},{4,2},{6,4},{8,6},{10,8},{12,10},{14,12},{16,14},{18,... | collective-permute-start | bytes 4718600 | tf_op jit(solution)/shard_map/while/body/eval_jaxpr/ppermute | solution.py:9
  170.9 1.9 copy-start
  173.8 27.6 %copy-start.1 = (f32[4,4,3,1,128,128]{4,5,1,0,3,2:T(8,128)}, f32[4,4,3,1,128,128]{4,5,1,0,3,2:T(8,128)S(1)}, u32[]{:S(2)}) copy-start(f32[4,4,3,1,128,128]{4,5,1,0,3,2:T(8,128)S(1)} %maximum_add_fusion.6) | copy-start | bytes 9437188 | tf_op jit(solution)/shard_map/while
  201.6 37.3 %collective-permute-start = (bf16[4,4,3,1,128,128]{5,4,2,1,0,3:T(8,128)(2,1)S(1)}, bf16[4,4,3,1,128,128]{5,4,2,1,0,3:T(8,128)(2,1)S(1)}, u32[]{:S(2)}, u32[]{:S(2)}) collective-permute-start(bf16[4,4,3,1,128,128]{5,4,2,1,0,3:T(8,128)(2,1)S(1)} %copy.62), channel_id=1, source_target_pairs={{0,30},{2,0},{4,2},{6,4},{8,6},{10,8},{12,10},{14,12},{16,14},{18,... | collective-permute-start | bytes 4718600 | tf_op jit(solution)/shard_map/while/body/eval_jaxpr/ppermute | solution.py:9
  209.2 1.9 copy-start
  212.2 26.6 %copy-start.1 = (f32[4,4,3,1,128,128]{4,5,1,0,3,2:T(8,128)}, f32[4,4,3,1,128,128]{4,5,1,0,3,2:T(8,128)S(1)}, u32[]{:S(2)}) copy-start(f32[4,4,3,1,128,128]{4,5,1,0,3,2:T(8,128)S(1)} %maximum_add_fusion.6) | copy-start | bytes 9437188 | tf_op jit(solution)/shard_map/while
  239.0 36.4 %collective-permute-start = (bf16[4,4,3,1,128,128]{5,4,2,1,0,3:T(8,128)(2,1)S(1)}, bf16[4,4,3,1,128,128]{5,4,2,1,0,3:T(8,128)(2,1)S(1)}, u32[]{:S(2)}, u32[]{:S(2)}) collective-permute-start(bf16[4,4,3,1,128,128]{5,4,2,1,0,3:T(8,128)(2,1)S(1)} %copy.62), channel_id=1, source_target_pairs={{0,30},{2,0},{4,2},{6,4},{8,6},{10,8},{12,10},{14,12},{16,14},{18,... | collective-permute-start | bytes 4718600 | tf_op jit(solution)/shard_map/while/body/eval_jaxpr/ppermute | solution.py:9
  246.7 1.9 copy-start
  249.7 25.7 %copy-start.1 = (f32[4,4,3,1,128,128]{4,5,1,0,3,2:T(8,128)}, f32[4,4,3,1,128,128]{4,5,1,0,3,2:T(8,128)S(1)}, u32[]{:S(2)}) copy-start(f32[4,4,3,1,128,128]{4,5,1,0,3,2:T(8,128)S(1)} %maximum_add_fusion.6) | copy-start | bytes 9437188 | tf_op jit(solution)/shard_map/while
  275.6 35.4 %collective-permute-start = (bf16[4,4,3,1,128,128]{5,4,2,1,0,3:T(8,128)(2,1)S(1)}, bf16[4,4,3,1,128,128]{5,4,2,1,0,3:T(8,128)(2,1)S(1)}, u32[]{:S(2)}, u32[]{:S(2)}) collective-permute-start(bf16[4,4,3,1,128,128]{5,4,2,1,0,3:T(8,128)(2,1)S(1)} %copy.62), channel_id=1, source_target_pairs={{0,30},{2,0},{4,2},{6,4},{8,6},{10,8},{12,10},{14,12},{16,14},{18,... | collective-permute-start | bytes 4718600 | tf_op jit(solution)/shard_map/while/body/eval_jaxpr/ppermute | solution.py:9
  283.3 1.9 copy-start
  286.2 24.8 %copy-start.1 = (f32[4,4,3,1,128,128]{4,5,1,0,3,2:T(8,128)}, f32[4,4,3,1,128,128]{4,5,1,0,3,2:T(8,128)S(1)}, u32[]{:S(2)}) copy-start(f32[4,4,3,1,128,128]{4,5,1,0,3,2:T(8,128)S(1)} %maximum_add_fusion.6) | copy-start | bytes 9437188 | tf_op jit(solution)/shard_map/while
  311.2 34.5 %collective-permute-start = (bf16[4,4,3,1,128,128]{5,4,2,1,0,3:T(8,128)(2,1)S(1)}, bf16[4,4,3,1,128,128]{5,4,2,1,0,3:T(8,128)(2,1)S(1)}, u32[]{:S(2)}, u32[]{:S(2)}) collective-permute-start(bf16[4,4,3,1,128,128]{5,4,2,1,0,3:T(8,128)(2,1)S(1)} %copy.62), channel_id=1, source_target_pairs={{0,30},{2,0},{4,2},{6,4},{8,6},{10,8},{12,10},{14,12},{16,14},{18,... | collective-permute-start | bytes 4718600 | tf_op jit(solution)/shard_map/while/body/eval_jaxpr/ppermute | solution.py:9
  318.9 1.9 copy-start
  321.9 23.9 %copy-start.1 = (f32[4,4,3,1,128,128]{4,5,1,0,3,2:T(8,128)}, f32[4,4,3,1,128,128]{4,5,1,0,3,2:T(8,128)S(1)}, u32[]{:S(2)}) copy-start(f32[4,4,3,1,128,128]{4,5,1,0,3,2:T(8,128)S(1)} %maximum_add_fusion.6) | copy-start | bytes 9437188 | tf_op jit(solution)/shard_map/while
  345.7 2.0 copy-start.8
  345.7 2.0 copy-start.10
  347.2 1.9 copy-start.2
  351.5 487.5 %all-reduce.6.cloned.1.call-start = ((), (), s32[]{:S(2)}) async-start(), calls=%async_computation.2 | async-start | bytes 6291456
  447.8 37.7 %collective-permute-start.3 = (bf16[4,4,3,1,128,128]{4,5,1,0,3,2:T(8,128)(2,1)S(1)}, bf16[4,4,3,1,128,128]{4,5,1,0,3,2:T(8,128)(2,1)}, u32[]{:S(2)}, u32[]{:S(2)}) collective-permute-start(bf16[4,4,3,1,128,128]{4,5,1,0,3,2:T(8,128)(2,1)S(1)} %get-tuple-element.405), channel_id=1, source_target_pairs={{0,16},{2,18},{4,20},{6,22},{8,24},{10,26},{12,28},{14,30},{16,0},... | collective-permute-start | bytes 4718600 | tf_op jit(solution)/shard_map/ppermute | solution.py:9
  486.8 37.7 %collective-permute-start.1 = (bf16[4,4,3,1,128,128]{5,4,2,1,0,3:T(8,128)(2,1)S(1)}, bf16[4,4,3,1,128,128]{5,4,2,1,0,3:T(8,128)(2,1)S(1)}, u32[]{:S(2)}, u32[]{:S(2)}) collective-permute-start(bf16[4,4,3,1,128,128]{5,4,2,1,0,3:T(8,128)(2,1)S(1)} %copy.72), channel_id=1, source_target_pairs={{0,30},{2,0},{4,2},{6,4},{8,6},{10,8},{12,10},{14,12},{16,14},{18,... | collective-permute-start | bytes 4718600 | tf_op jit(solution)/shard_map/while/body/eval_jaxpr/ppermute | solution.py:9
  493.5 1.9 copy-start.3
  496.5 28.0 %copy-start.4 = (f32[4,4,3,1,128,128]{4,5,1,0,3,2:T(8,128)}, f32[4,4,3,1,128,128]{4,5,1,0,3,2:T(8,128)S(1)}, u32[]{:S(2)}) copy-start(f32[4,4,3,1,128,128]{4,5,1,0,3,2:T(8,128)S(1)} %maximum_add_fusion.7) | copy-start | bytes 9437188 | tf_op jit(solution)/shard_map/while
  524.7 37.7 %collective-permute-start.1 = (bf16[4,4,3,1,128,128]{5,4,2,1,0,3:T(8,128)(2,1)S(1)}, bf16[4,4,3,1,128,128]{5,4,2,1,0,3:T(8,128)(2,1)S(1)}, u32[]{:S(2)}, u32[]{:S(2)}) collective-permute-start(bf16[4,4,3,1,128,128]{5,4,2,1,0,3:T(8,128)(2,1)S(1)} %copy.72), channel_id=1, source_target_pairs={{0,30},{2,0},{4,2},{6,4},{8,6},{10,8},{12,10},{14,12},{16,14},{18,... | collective-permute-start | bytes 4718600 | tf_op jit(solution)/shard_map/while/body/eval_jaxpr/ppermute | solution.py:9
  532.3 1.9 copy-start.3
  535.3 27.1 %copy-start.4 = (f32[4,4,3,1,128,128]{4,5,1,0,3,2:T(8,128)}, f32[4,4,3,1,128,128]{4,5,1,0,3,2:T(8,128)S(1)}, u32[]{:S(2)}) copy-start(f32[4,4,3,1,128,128]{4,5,1,0,3,2:T(8,128)S(1)} %maximum_add_fusion.7) | copy-start | bytes 9437188 | tf_op jit(solution)/shard_map/while
  562.6 36.8 %collective-permute-start.1 = (bf16[4,4,3,1,128,128]{5,4,2,1,0,3:T(8,128)(2,1)S(1)}, bf16[4,4,3,1,128,128]{5,4,2,1,0,3:T(8,128)(2,1)S(1)}, u32[]{:S(2)}, u32[]{:S(2)}) collective-permute-start(bf16[4,4,3,1,128,128]{5,4,2,1,0,3:T(8,128)(2,1)S(1)} %copy.72), channel_id=1, source_target_pairs={{0,30},{2,0},{4,2},{6,4},{8,6},{10,8},{12,10},{14,12},{16,14},{18,... | collective-permute-start | bytes 4718600 | tf_op jit(solution)/shard_map/while/body/eval_jaxpr/ppermute | solution.py:9
  570.2 1.9 copy-start.3
  573.2 26.2 %copy-start.4 = (f32[4,4,3,1,128,128]{4,5,1,0,3,2:T(8,128)}, f32[4,4,3,1,128,128]{4,5,1,0,3,2:T(8,128)S(1)}, u32[]{:S(2)}) copy-start(f32[4,4,3,1,128,128]{4,5,1,0,3,2:T(8,128)S(1)} %maximum_add_fusion.7) | copy-start | bytes 9437188 | tf_op jit(solution)/shard_map/while
  599.6 35.9 %collective-permute-start.1 = (bf16[4,4,3,1,128,128]{5,4,2,1,0,3:T(8,128)(2,1)S(1)}, bf16[4,4,3,1,128,128]{5,4,2,1,0,3:T(8,128)(2,1)S(1)}, u32[]{:S(2)}, u32[]{:S(2)}) collective-permute-start(bf16[4,4,3,1,128,128]{5,4,2,1,0,3:T(8,128)(2,1)S(1)} %copy.72), channel_id=1, source_target_pairs={{0,30},{2,0},{4,2},{6,4},{8,6},{10,8},{12,10},{14,12},{16,14},{18,... | collective-permute-start | bytes 4718600 | tf_op jit(solution)/shard_map/while/body/eval_jaxpr/ppermute | solution.py:9
  607.2 1.9 copy-start.3
  610.2 25.2 %copy-start.4 = (f32[4,4,3,1,128,128]{4,5,1,0,3,2:T(8,128)}, f32[4,4,3,1,128,128]{4,5,1,0,3,2:T(8,128)S(1)}, u32[]{:S(2)}) copy-start(f32[4,4,3,1,128,128]{4,5,1,0,3,2:T(8,128)S(1)} %maximum_add_fusion.7) | copy-start | bytes 9437188 | tf_op jit(solution)/shard_map/while
  635.6 35.0 %collective-permute-start.1 = (bf16[4,4,3,1,128,128]{5,4,2,1,0,3:T(8,128)(2,1)S(1)}, bf16[4,4,3,1,128,128]{5,4,2,1,0,3:T(8,128)(2,1)S(1)}, u32[]{:S(2)}, u32[]{:S(2)}) collective-permute-start(bf16[4,4,3,1,128,128]{5,4,2,1,0,3:T(8,128)(2,1)S(1)} %copy.72), channel_id=1, source_target_pairs={{0,30},{2,0},{4,2},{6,4},{8,6},{10,8},{12,10},{14,12},{16,14},{18,... | collective-permute-start | bytes 4718600 | tf_op jit(solution)/shard_map/while/body/eval_jaxpr/ppermute | solution.py:9
  643.3 1.9 copy-start.3
  646.3 24.3 %copy-start.4 = (f32[4,4,3,1,128,128]{4,5,1,0,3,2:T(8,128)}, f32[4,4,3,1,128,128]{4,5,1,0,3,2:T(8,128)S(1)}, u32[]{:S(2)}) copy-start(f32[4,4,3,1,128,128]{4,5,1,0,3,2:T(8,128)S(1)} %maximum_add_fusion.7) | copy-start | bytes 9437188 | tf_op jit(solution)/shard_map/while
  670.8 34.4 %collective-permute-start.1 = (bf16[4,4,3,1,128,128]{5,4,2,1,0,3:T(8,128)(2,1)S(1)}, bf16[4,4,3,1,128,128]{5,4,2,1,0,3:T(8,128)(2,1)S(1)}, u32[]{:S(2)}, u32[]{:S(2)}) collective-permute-start(bf16[4,4,3,1,128,128]{5,4,2,1,0,3:T(8,128)(2,1)S(1)} %copy.72), channel_id=1, source_target_pairs={{0,30},{2,0},{4,2},{6,4},{8,6},{10,8},{12,10},{14,12},{16,14},{18,... | collective-permute-start | bytes 4718600 | tf_op jit(solution)/shard_map/while/body/eval_jaxpr/ppermute | solution.py:9
  678.4 1.9 copy-start.3
  681.4 23.7 %copy-start.4 = (f32[4,4,3,1,128,128]{4,5,1,0,3,2:T(8,128)}, f32[4,4,3,1,128,128]{4,5,1,0,3,2:T(8,128)S(1)}, u32[]{:S(2)}) copy-start(f32[4,4,3,1,128,128]{4,5,1,0,3,2:T(8,128)S(1)} %maximum_add_fusion.7) | copy-start | bytes 9437188 | tf_op jit(solution)/shard_map/while
  705.3 33.2 %collective-permute-start.1 = (bf16[4,4,3,1,128,128]{5,4,2,1,0,3:T(8,128)(2,1)S(1)}, bf16[4,4,3,1,128,128]{5,4,2,1,0,3:T(8,128)(2,1)S(1)}, u32[]{:S(2)}, u32[]{:S(2)}) collective-permute-start(bf16[4,4,3,1,128,128]{5,4,2,1,0,3:T(8,128)(2,1)S(1)} %copy.72), channel_id=1, source_target_pairs={{0,30},{2,0},{4,2},{6,4},{8,6},{10,8},{12,10},{14,12},{16,14},{18,... | collective-permute-start | bytes 4718600 | tf_op jit(solution)/shard_map/while/body/eval_jaxpr/ppermute | solution.py:9
  713.0 1.9 copy-start.3
  716.0 22.5 %copy-start.4 = (f32[4,4,3,1,128,128]{4,5,1,0,3,2:T(8,128)}, f32[4,4,3,1,128,128]{4,5,1,0,3,2:T(8,128)S(1)}, u32[]{:S(2)}) copy-start(f32[4,4,3,1,128,128]{4,5,1,0,3,2:T(8,128)S(1)} %maximum_add_fusion.7) | copy-start | bytes 9437188 | tf_op jit(solution)/shard_map/while
  738.5 1.5 copy-start.9
  738.5 1.5 copy-start.11
  740.0 1.9 copy-start.5
  744.3 0.7 copy-start.13
  744.3 94.7 %copy-start.7 = (f32[4,4,3,1,128,128]{4,5,1,0,3,2:T(8,128)S(1)}, f32[4,4,3,1,128,128]{4,5,1,0,3,2:T(8,128)}, u32[]{:S(2)}) copy-start(f32[4,4,3,1,128,128]{4,5,1,0,3,2:T(8,128)} %get-tuple-element.406) | copy-start | bytes 9437188
Sparse Core Ops, SparseCore 0:
  11.5 70.8 all-gather.1
  351.6 92.0 all-reduce.3
  744.4 94.5 all-reduce.5
where the time goes:
time: 853 us; the launch traced here: 851 us
  waiting for transfers between devices  644 us (75%)
  starting transfers between devices  86.7 us (10%)
  local copies, waits for them, and re-layouts  48.5 us (6%)
  other arithmetic  29.9 us (4%)
  matrix products  27.2 us (3%)
  between operations  13.9 us (2%)
    ppermute x16, waiting for transfers between devices, shifted_2(): lax.ppermute(array, axis, [(i, (i + by) % length) for i in range(length)])  433 us
    unnamed x4, waiting for transfers between devices  92.9 us
    psum x1, waiting for transfers between devices, local(): square = lax.psum(product(masked[1:region_count + 1]), 'layer') * kept_rows  92 us
    ppermute x16, starting transfers between devices, shifted_2(): lax.ppermute(array, axis, [(i, (i + by) % length) for i in range(length)])  86.6 us
    dot_general x48, matrix products, contract(): jnp.einsum('brdcxy,bdcwyz->brwxz', left_stack, right_stack, preferred_ele...  27.2 us
    all_gather x1, waiting for transfers between devices, local(): panel_all = lax.all_gather(masked, 'row', axis=1, tiled=True)  26.9 us
    slice x15, local copies, waits for them, and re-layouts, contract(): right_blocks[d_index:d_index + region_count, :, e_index - d_index + 1]  20.5 us
  transfers between devices with their start and end apart: 19, of which 19 were waited for; matrix products, arithmetic and copies ran while one was open for 7% of the time, Pallas kernels for 0%

commit v1 on v0

v1 whole, which is shorter than its diff:
```python
import functools

import jax
import jax.numpy as jnp
from jax import lax
from jax.experimental import pallas as pl
from jax.experimental.pallas import tpu as pltpu
from jax.sharding import PartitionSpec as P

MESH = pl.DeviceIdType.MESH
BF, F32 = jnp.bfloat16, jnp.float32
N_SEMS = 96


def kernel(
    x_ref, pres_ref, out_ref,
    xm, pmask, pmask_in, left, sq, right, sq32, acc, osend, orecv,
    send_sems, recv_sems, local_sems,
):
    row, col, zl = lax.axis_index("row"), lax.axis_index("col"), lax.axis_index("layer")
    zh, co = row // 2, row % 2
    y, x = col // 4, col % 4
    z = 2 * zh + zl

    def flip1(v):
        return v + 1 - 2 * (v % 2)

    def flip2(v):
        return (v + 2) % 4

    def flip3(v):
        return 3 - v

    def device(z_, y_, x_, co_):
        return (2 * (z_ // 2) + co_, 4 * y_ + x_, z_ % 2)

    xi = device(z, y, flip1(x), co)
    xo = device(z, y, flip3(x), co)
    y1 = device(z, flip1(y), x, co)
    y3 = device(z, flip3(y), x, co)
    zo = device(flip3(z), y, x, co)
    z2 = device(flip2(z), y, x, co)
    sib = device(z, y, x, 1 - co)
    partners = (xi, xo, y1, y3, zo, z2, sib)

    barrier = pltpu.get_barrier_semaphore()
    for partner in partners:
        pl.semaphore_signal(barrier, inc=1, device_id=partner, device_id_type=MESH)

    beta = ((x + 1) // 2) % 2
    b = 2 * zl + beta
    b_xi = 2 * zl + 1 - beta
    b_zo = 2 * (1 - zl) + beta
    my_col = 4 * y + x
    pair_col = 4 * y + flip1(x)
    my_kg = row
    zo_kg = 2 * (1 - zh) + co

    def mask_region(q, carry):
        for a in range(4):
            for o in range(3):
                kept = pres_ref[q * 12 + a * 3 + o].astype(F32)
                xm[q, a, o] = (x_ref[q, a, o].astype(F32) * kept).astype(BF)
                pmask[q, a * 3 + o] = jnp.full((128,), 1.0, F32) * kept
        for i in range(12, 16):
            pmask[q, i] = jnp.zeros((128,), F32)
        return carry

    lax.fori_loop(0, 6, mask_region, 0)
    pl.semaphore_wait(barrier, len(partners))

    started = []

    def send(src, dst, to):
        i = len(started)
        copy = pltpu.make_async_remote_copy(
            src_ref=src, dst_ref=dst, send_sem=send_sems.at[i], recv_sem=recv_sems.at[i],
            device_id=to, device_id_type=MESH,
        )
        copy.start()
        started.append(copy)
        return copy

    def gather(buf, r0, nr, p_src, q_ready):
        half = nr // 2
        full = pl.ds(r0, nr)
        part_a, part_b = pl.ds(r0, half), pl.ds(r0 + half, half)
        y1c, y2c, y3c = 4 * flip1(y), 4 * flip2(y), 4 * flip3(y)
        yc = 4 * y
        d0, d1, d2, d3 = x, flip1(x), flip2(x), flip3(x)

        def piece(c, rows, to):
            ref = buf.at[c, rows]
            return send(ref, ref, to)

        def own(to):
            return send(p_src, buf.at[my_col, full], to)

        p_xo, p_y1, p_y3 = own(xo), own(y1), own(y3)
        yield
        q_ready()
        q_y1, q_y3, q_xo = (piece(pair_col, full, t) for t in (y1, y3, xo))
        yield
        p_xo.wait_recv()
        r_y1, r_y3 = piece(yc + d3, full, y1), piece(yc + d3, full, y3)
        p_y1.wait_recv()
        p_a = piece(y1c + d0, part_a, y3)
        p_y3.wait_recv()
        p_b = piece(y3c + d0, part_b, y1)
        yield
        q_y1.wait_recv()
        q_a, s_1 = piece(y1c + d1, part_a, y3), piece(y1c + d1, full, xo)
        q_y3.wait_recv()
        q_b, s_3 = piece(y3c + d1, part_b, y1), piece(y3c + d1, full, xo)
        yield
        r_y1.wait_recv()
        r_a = piece(y1c + d3, part_a, y3)
        r_y3.wait_recv()
        r_b = piece(y3c + d3, part_b, y1)
        yield
        q_a.wait_recv()
        s_a = piece(y2c + d1, part_a, xo)
        q_b.wait_recv()
        s_b = piece(y2c + d1, part_b, xo)
        yield
        for copy in (p_a, p_b, q_xo, r_a, r_b, s_1, s_3, s_a, s_b):
            copy.wait_recv()

    def finish(stages):
        for _ in stages:
            pass

    l_xi = send(xm.at[b_xi + 1], left.at[my_col], xi)
    mask_xi = send(pmask.at[b_xi + 1], pmask_in, xi)
    z_mid = send(xm.at[b_zo + 1], right.at[0, my_kg, 1], zo)
    panel = gather(left, 0, 4, xm.at[b + 1], l_xi.wait_recv)
    next(panel)
    z_low = send(xm.at[b_zo], right.at[0, my_kg, 0], zo)
    z_high = send(xm.at[b_zo + 2], right.at[0, my_kg, 2], zo)
    c_own = send(xm.at[pl.ds(b, 3)], right.at[0, my_kg], sib)
    own_left = pltpu.make_async_copy(xm.at[b + 1], left.at[my_col], local_sems.at[0])
    own_left.start()
    own_right = pltpu.make_async_copy(xm.at[pl.ds(b, 3)], right.at[0, my_kg], local_sems.at[1])
    own_right.start()
    next(panel)
    two_xi = send(xm.at[pl.ds(b_xi + 1 - beta, 2)], right.at[1, my_kg, pl.ds(1 - beta, 2)], xi)
    one_xi = send(xm.at[b_xi + 2 * beta], right.at[1, my_kg, 2 * beta], xi)
    next(panel)
    z_mid.wait_recv()
    c_mid = send(right.at[0, zo_kg, 1], right.at[0, zo_kg, 1], sib)
    diag_xi = send(right.at[0, zo_kg, 1], right.at[1, zo_kg, 2 * beta], xi)
    next(panel)
    next(panel)
    two = right.at[1, my_kg, pl.ds(beta, 2)]
    two_xi.wait_recv()
    diag_z = send(two, two, z2)
    c_two = send(two, two, sib)
    next(panel)
    z_low.wait_recv()
    c_low = send(right.at[0, zo_kg, 0], right.at[0, zo_kg, 0], sib)
    z_high.wait_recv()
    c_high = send(right.at[0, zo_kg, 2], right.at[0, zo_kg, 2], sib)
    one_at = right.at[1, my_kg, 2 - 2 * beta]
    one_xi.wait_recv()
    c_one = send(one_at, one_at, sib)
    diag_at = right.at[1, zo_kg, 2 - 2 * beta]
    diag_xi.wait_recv()
    c_diag_xi = send(diag_at, diag_at, sib)
    zdiag_at = right.at[1, zo_kg, pl.ds(beta, 2)]
    diag_z.wait_recv()
    c_diag_z = send(zdiag_at, zdiag_at, sib)
    finish(panel)
    own_left.wait()
    own_right.wait()
    mask_xi.wait_recv()
    for copy in (c_own, c_mid, c_two, c_low, c_high, c_one, c_diag_xi, c_diag_z):
        copy.wait_recv()

    def product(buf, r0):
        for e in range(3):
            offsets = [d for d in range(3) if 0 <= e - d + 1 <= 2]

            def group(kg, carry):
                lhs = jnp.concatenate(
                    [
                        buf[4 * kg + k, r0 : r0 + 2, d].reshape(256, 128)
                        for d in offsets for k in range(4)
                    ],
                    axis=1,
                )
                rhs = jnp.concatenate(
                    [
                        jnp.concatenate([right[j, kg, d, k, e - d + 1] for j in range(2)], axis=1)
                        for d in offsets for k in range(4)
                    ],
                    axis=0,
                )
                acc[e] += jnp.dot(lhs, rhs, preferred_element_type=F32)
                return carry

            acc[e] = jnp.zeros((256, 256), F32)
            lax.fori_loop(0, 4, group, 0)

    def kept(j, a, e):
        i = a * 3 + e
        return (pmask[b + 1, i : i + 1] if j == 0 else pmask_in[i : i + 1])

    def square_rows(r0):
        product(left, r0)
        for a in range(2):
            for e in range(3):
                for j, c in ((0, my_col), (1, pair_col)):
                    block = acc[e, a * 128 : a * 128 + 128, j * 128 : j * 128 + 128]
                    block = block * kept(j, r0 + a, e)
                    sq32[j, r0 + a, e] = block
                    sq[c, r0 + a, e] = block.astype(BF)

    def result_rows(r0):
        product(sq, r0)
        for a in range(2):
            for e in range(3):
                for j in range(2):
                    block = acc[e, a * 128 : a * 128 + 128, j * 128 : j * 128 + 128]
                    block = 3.0 * sq32[j, r0 + a, e] - 2.0 * (block * kept(j, r0 + a, e))
                    if j == 0:
                        out_ref[beta, r0 + a, e] = block.astype(BF)
                    else:
                        osend[r0 + a, e] = block.astype(BF)
        return send(osend.at[pl.ds(r0, 2)], orecv.at[pl.ds(r0, 2)], xi)

    gathers = []
    for r0 in (0, 2):
        square_rows(r0)
        stages = gather(sq, r0, 2, sq.at[my_col, pl.ds(r0, 2)], lambda: None)
        next(stages)
        next(stages)
        gathers.append(stages)
    first, second = gathers
    next(first)
    next(first)
    next(second)
    next(first)
    next(first)
    next(second)
    finish(first)
    next(second)
    out_first = result_rows(0)
    finish(second)
    out_second = result_rows(2)
    for r0, copy in ((0, out_first), (2, out_second)):
        copy.wait_recv()
        out_ref[1 - beta, r0 : r0 + 2] = orecv[r0 : r0 + 2]
    for copy in started:
        copy.wait_send()


def local(x_blocks, present):
    block = jax.ShapeDtypeStruct
    x = x_blocks.reshape(6, 4, 3, 128, 128)
    purified = pl.pallas_call(
        kernel,
        out_shape=block((2, 4, 3, 128, 128), BF),
        in_specs=[pl.BlockSpec(memory_space=pltpu.VMEM), pl.BlockSpec(memory_space=pltpu.SMEM)],
        out_specs=pl.BlockSpec(memory_space=pltpu.VMEM),
        scratch_shapes=[
            pltpu.VMEM((6, 4, 3, 128, 128), BF),
            pltpu.VMEM((6, 16, 128), F32),
            pltpu.VMEM((16, 128), F32),
            pltpu.VMEM((16, 4, 3, 128, 128), BF),
            pltpu.VMEM((16, 4, 3, 128, 128), BF),
            pltpu.VMEM((2, 4, 3, 4, 3, 128, 128), BF),
            pltpu.VMEM((2, 4, 3, 128, 128), F32),
            pltpu.VMEM((3, 256, 256), F32),
            pltpu.VMEM((4, 3, 128, 128), BF),
            pltpu.VMEM((4, 3, 128, 128), BF),
            pltpu.SemaphoreType.DMA((N_SEMS,)),
            pltpu.SemaphoreType.DMA((N_SEMS,)),
            pltpu.SemaphoreType.DMA((2,)),
        ],
        compiler_params=pltpu.CompilerParams(
            collective_id=0, has_side_effects=True, vmem_limit_bytes=56 * 2**20
        ),
        cost_estimate=pl.CostEstimate(flops=7_500_000_000, bytes_accessed=4_000_000, transcendentals=0),
    )(x, present.reshape(72))
    return purified.astype(F32).reshape(2, 4, 3, 1, 128, 128)


def solution(mesh):
    return jax.shard_map(
        local,
        mesh=mesh,
        in_specs=(P(None, "row", None, "col", None, None), P(None, "row", None, "col")),
        out_specs=P("layer", "row", None, "col", None, None),
        check_vma=False,
    )
```

time: 853 us -> 121 us (0.14)
  waiting for transfers between devices: 644 us -> 0 us
  Pallas kernels: 0 us -> 115 us
  starting transfers between devices: 86.7 us -> 0 us
  local copies, waits for them, and re-layouts: 48.5 us -> 1.41 us
  other arithmetic: 29.9 us -> 2.45 us
  matrix products: 27.2 us -> 0 us
  between operations: 13.9 us -> 0.01 us
    ppermute x16 -> x0, waiting for transfers between devices: 433 us -> none  [shifted_2(): lax.ppermute(array, axis, [(i, (i + by) % length) for i in range(length)])]
    pallas_call x0 -> x1, Pallas kernels: none -> 115 us  [local(): pl.pallas_call(kernel, out_shape=block((2, 4, 3, 128, 128), BF), in_specs...]
    unnamed x4 -> x0, waiting for transfers between devices: 92.9 us -> none
    psum x1 -> x0, waiting for transfers between devices: 92 us -> none  [local(): square = lax.psum(product(masked[1:region_count + 1]), 'layer') * kept_rows]
    ppermute x16 -> x0, starting transfers between devices: 86.6 us -> none  [shifted_2(): lax.ppermute(array, axis, [(i, (i + by) % length) for i in range(length)])]
    dot_general x48 -> x0, matrix products: 27.2 us -> none  [contract(): jnp.einsum('brdcxy,bdcwyz->brwxz', left_stack, right_stack, preferred_ele...]
    all_gather x1 -> x0, waiting for transfers between devices: 26.9 us -> none  [local(): panel_all = lax.all_gather(masked, 'row', axis=1, tiled=True)]
    slice x17 -> x0, local copies, waits for them, and re-layouts: 21.8 us -> none  [the longest x15 20.5 us: contract(): right_blocks[d_index:d_index + region_count, :, e_index - d_index + 1]]
  transfers between devices with their start and end apart: 19 -> 0, of which waited for: 19 -> 0; matrix products, arithmetic and copies ran while one was open for 7% -> 0% of each run, Pallas kernels for 0% -> 0%
where the time goes in v1:
time: 121 us; the launch traced here: 119 us
  Pallas kernels  115 us (95%)
  other arithmetic  2.45 us (2%)
  local copies, waits for them, and re-layouts  1.41 us (1%)
    pallas_call x1, Pallas kernels, local(): pl.pallas_call(kernel, out_shape=block((2, 4, 3, 128, 128), BF), in_specs...  115 us
    reshape x1, other arithmetic, local(): return purified.astype(F32).reshape(2, 4, 3, 1, 128, 128)  2.45 us

profile of v1, /device:TPU:0, one launch (start us, length us, event | category | flops | bytes accessed | tf_op | source)
XLA Modules:
  0.0 119.0 jit_solution(3130267489112507453)
XLA Ops:
  0.0 0.8 copy.5
  0.8 0.6 reshape.13.pres_ref
  1.4 115.2 %shard_map.28 = bf16[2,4,3,128,128]{4,3,2,1,0:T(8,128)(2,1)} custom-call(bf16[6,4,3,128,128]{4,3,2,1,0:T(8,128)(2,1)} %bitcast.9, s32[72]{0:T(128)} %reshape.13.pres_ref), custom_call_target="tpu_custom_call" | custom-call | flops 7500000256 | bytes 4000000 | tf_op jit(solution)/shard_map/pallas_call | solution.py:260
  116.6 2.5 %bitcast_convert_fusion = f32[2,4,3,1,128,128]{5,4,3,2,1,0:T(8,128)} fusion(bf16[2,4,3,128,128]{4,3,2,1,0:T(8,128)(2,1)} %shard_map.28), kind=kLoop, calls=%fused_computation | loop fusion | flops 393216 | bytes 2359296 | tf_op jit(solution)/shard_map/reshape | solution.py:285

commit v2 on v0

v2 whole, which is shorter than its diff:
```python
import jax
import jax.numpy as jnp
from jax import lax
from jax.experimental import pallas as pl
from jax.experimental.pallas import tpu as pltpu
from jax.sharding import PartitionSpec as P

MESH = pl.DeviceIdType.MESH
BF, F32 = jnp.bfloat16, jnp.float32
N_SEMS = 96
C0, C1, C2, C3 = 0, 1, 2, 3


def kernel(
    x_ref, pres_ref, out_ref,
    xr, pmask, pmask_in, left, sq, right, sq32, acc_a, acc_b, acc_c, cube, osend, orecv,
    send_sems, recv_sems, local_sems,
):
    row, col, zl = lax.axis_index("row"), lax.axis_index("col"), lax.axis_index("layer")
    zh, co = row // 2, row % 2
    y, x = col // 4, col % 4
    z = 2 * zh + zl

    def flip1(v):
        return v + 1 - 2 * (v % 2)

    def flip2(v):
        return (v + 2) % 4

    def flip3(v):
        return 3 - v

    def device(z_, y_, x_, co_):
        return (2 * (z_ // 2) + co_, 4 * y_ + x_, z_ % 2)

    columns = (x, flip1(x), flip2(x), flip3(x))
    y1c, y2c, y3c = flip1(y), flip2(y), flip3(y)
    xi, x2, xo = (device(z, y, c, co) for c in columns[1:])
    y1 = device(z, y1c, x, co)
    y3 = device(z, y3c, x, co)
    zo = device(flip3(z), y, x, co)
    z2 = device(flip2(z), y, x, co)
    sib = device(z, y, x, 1 - co)
    partners = (xi, x2, xo, y1, y3, zo, z2, sib)

    barrier = pltpu.get_barrier_semaphore()
    for partner in partners:
        pl.semaphore_signal(barrier, inc=1, device_id=partner, device_id_type=MESH)

    beta, rho = x // 2, x % 2
    b = 2 * zl + beta
    b_xo = 2 * zl + 1 - beta
    b_zo = 2 * (1 - zl) + beta
    rows = 2 * rho
    rows_flip = 2 - rows
    kg0 = row
    kg1 = 2 * (1 - zh) + co
    m_at, e_at = 3 * (1 - beta), 4 * beta
    m_xo, e_xo = 3 * beta, 4 * (1 - beta)

    def mask_region(q, carry):
        for a in range(4):
            for o in range(3):
                keep = pres_ref[q * 12 + a * 3 + o].astype(F32)
                xr[3 * q + o, a] = (x_ref[q, a, o].astype(F32) * keep).astype(BF)
                pmask[q, a * 3 + o] = jnp.full((128,), 1.0, F32) * keep
        for i in range(12, 16):
            pmask[q, i] = jnp.zeros((128,), F32)
        return carry

    lax.fori_loop(0, 6, mask_region, 0)
    pl.semaphore_wait(barrier, len(partners))

    started = []

    def send(src, dst, to):
        i = len(started)
        copy = pltpu.make_async_remote_copy(
            src_ref=src, dst_ref=dst, send_sem=send_sems.at[i], recv_sem=recv_sems.at[i],
            device_id=to, device_id_type=MESH,
        )
        copy.start()
        started.append(copy)
        return copy

    def same(ref, to):
        return send(ref, ref, to)

    class Ring:
        def __init__(self, buf, j, src=None):
            self.buf, self.c = buf, columns[j]
            at = buf.at[4 * y + self.c]
            src = at if src is None else src
            self.y1, self.y3 = send(src, at, y1), send(src, at, y3)

        def relay(self):
            self.y1.wait_recv()
            self.a = same(self.buf.at[4 * y1c + self.c, :, pl.ds(0, 1)], y3)
            self.y3.wait_recv()
            self.b = same(self.buf.at[4 * y3c + self.c, :, pl.ds(1, 1)], y1)

        def wait(self):
            self.a.wait_recv()
            self.b.wait_recv()

    def left_of(region, first_row):
        return xr.at[pl.ds(3 * region + 3, 3), pl.ds(first_row, 2)]

    my_left = left.at[4 * y + x]
    own_left_src = left_of(b, rows)
    lp1 = send(left_of(b, rows_flip), my_left, xi)
    lp3 = send(left_of(b_xo, rows_flip), my_left, xo)
    lp2 = send(left_of(b_xo, rows), my_left, x2)
    l0 = Ring(left, C0, own_left_src)
    own_left = pltpu.make_async_copy(own_left_src, my_left, local_sems.at[0])
    own_left.start()

    def native(region, at, size):
        return xr.at[pl.ds(3 * region + 1 + at, size)]

    def panel(j, kg, at=None, size=7):
        return right.at[j, kg] if at is None else right.at[j, kg, pl.ds(at, size)]

    b_m = send(native(b_zo, m_at, 4), panel(C0, kg0, m_at, 4), zo)
    b_e = send(native(b_zo, e_at, 3), panel(C0, kg0, e_at, 3), zo)
    c_e = send(native(b_xo, e_xo, 3), panel(C3, kg0, e_xo, 3), xo)
    a_7 = send(native(b, 0, 7), panel(C1, kg0), xi)
    sib_0 = send(native(b, 0, 7), panel(C0, kg0), sib)
    own_right = pltpu.make_async_copy(native(b, 0, 7), panel(C0, kg0), local_sems.at[1])
    own_right.start()
    masks = [send(pmask.at[bb + 1], pmask_in.at[i], to) for i, (bb, to) in enumerate(((b, xi), (b_xo, x2), (b_xo, xo)))]

    lp1.wait_recv()
    l1 = Ring(left, C1)
    lp3.wait_recv()
    l3 = Ring(left, C3)
    l0.relay()
    lp2.wait_recv()
    l2 = Ring(left, C2)

    b_m.wait_recv()
    g_m = send(panel(C0, kg1, m_at, 4), panel(C3, kg1, m_xo, 4), xo)
    sib_b_m = same(panel(C0, kg1, m_at, 4), sib)
    c_e.wait_recv()
    c_m = send(native(b_xo, m_xo, 4), panel(C3, kg0, m_xo, 4), xo)
    h_e = same(panel(C3, kg0, e_at, 3), z2)
    sib_c_e = same(panel(C3, kg0, e_at, 3), sib)
    l1.relay()
    l3.relay()
    b_e.wait_recv()
    sib_b_e = same(panel(C0, kg1, e_at, 3), sib)
    l2.relay()
    a_7.wait_recv()
    d_7 = same(panel(C1, kg0), z2)
    f_m = send(panel(C1, kg0, m_at, 4), panel(C2, kg0, m_xo, 4), xo)
    sib_a = same(panel(C1, kg0), sib)
    g_m.wait_recv()
    i_m = send(panel(C3, kg1, m_at, 4), panel(C2, kg1, m_at, 4), xi)
    sib_g = same(panel(C3, kg1, m_at, 4), sib)
    e_e = send(panel(C3, kg0, e_at, 3), panel(C2, kg0, e_at, 3), xi)
    h_e.wait_recv()
    i_e = send(panel(C3, kg1, e_at, 3), panel(C2, kg1, e_at, 3), xi)
    sib_h = same(panel(C3, kg1, e_at, 3), sib)

    def square_column(j):
        def lhs(kg, d):
            return jnp.concatenate([left[4 * kg + k, d].reshape(256, 128) for k in range(4)], axis=1)

        def block(kg, g):
            return right[j, kg, g].reshape(512, 128)

        acc_a[...] = jnp.zeros_like(acc_a)
        acc_b[...] = jnp.zeros_like(acc_b)
        acc_c[...] = jnp.zeros_like(acc_c)

        def group(kg, carry):
            l_0, l_1, l_2 = lhs(kg, 0), lhs(kg, 1), lhs(kg, 2)
            r = [block(kg, g) for g in range(7)]
            acc_a[...] += jnp.dot(
                jnp.concatenate([l_0, l_1], axis=1),
                jnp.concatenate(
                    [jnp.concatenate([r[0], r[1]], axis=1), jnp.concatenate([r[2], r[3]], axis=1)], axis=0
                ),
                preferred_element_type=F32,
            )
            acc_b[...] += jnp.dot(l_2, jnp.concatenate([r[5], r[6]], axis=1), preferred_element_type=F32)
            acc_c[...] += jnp.dot(l_1, r[4], preferred_element_type=F32)
            return carry

        lax.fori_loop(0, 4, group, 0)
        out = (
            acc_a[:, :128],
            acc_a[:, 128:] + acc_b[:, :128],
            acc_b[:, 128:] + acc_c[...],
        )
        for e in range(3):
            for a in range(2):
                block = out[e][a * 128 : a * 128 + 128] * kept(j, a, e)
                sq32[j, e, a] = block
                sq[4 * y + columns[j], e, a] = block.astype(BF)
        return Ring(sq, j)

    def kept(j, a, e):
        i = (rows + a) * 3 + e
        return pmask[b + 1, pl.ds(i, 1)] if j == 0 else pmask_in[j - 1, pl.ds(i, 1)]

    def cube_part(j, first):
        c = columns[j]
        for e in range(3):
            offsets = [d for d in range(3) if 0 <= e - d + 1 <= 2]
            lhs = jnp.concatenate(
                [sq[4 * yy + c, d].reshape(256, 128) for d in offsets for yy in range(4)], axis=1
            )
            for half in range(2):
                rhs = jnp.concatenate(
                    [
                        jnp.concatenate([right[2 * half + i, yy, 2 * d + e, c] for i in range(2)], axis=1)
                        for d in offsets for yy in range(4)
                    ],
                    axis=0,
                )
                part = jnp.dot(lhs, rhs, preferred_element_type=F32)
                if first:
                    cube[e, half] = part
                else:
                    cube[e, half] += part

    for copy in masks:
        copy.wait_recv()
    l0.wait()
    l1.wait()
    l3.wait()
    l2.wait()
    own_left.wait()
    own_right.wait()
    for copy in (sib_0, sib_b_m, sib_b_e):
        copy.wait_recv()
    s0 = square_column(C0)
    c_m.wait_recv()
    sib_c_m = same(panel(C3, kg0, m_at, 4), sib)
    for copy in (sib_g, sib_h, sib_c_e, sib_c_m):
        copy.wait_recv()
    s3 = square_column(C3)
    s0.relay()
    d_7.wait_recv()
    sib_d = same(panel(C1, kg1), sib)
    f_m.wait_recv()
    sib_f = same(panel(C2, kg0, m_at, 4), sib)
    sib_a.wait_recv()
    sib_d.wait_recv()
    s1 = square_column(C1)
    s3.relay()
    i_m.wait_recv()
    sib_i_m = same(panel(C2, kg1, m_at, 4), sib)
    e_e.wait_recv()
    sib_e = same(panel(C2, kg0, e_at, 3), sib)
    i_e.wait_recv()
    sib_i_e = same(panel(C2, kg1, e_at, 3), sib)
    for copy in (sib_f, sib_e, sib_i_m, sib_i_e):
        copy.wait_recv()
    s2 = square_column(C2)
    s1.relay()
    s0.wait()
    cube_part(C0, True)
    s2.relay()
    s3.wait()
    cube_part(C3, False)
    s1.wait()
    cube_part(C1, False)
    s2.wait()
    cube_part(C2, False)

    outs = []
    for j in (2, 1, 3, 0):
        for e in range(3):
            for a in range(2):
                block = cube[e, j // 2, a * 128 : a * 128 + 128, (j % 2) * 128 : (j % 2) * 128 + 128]
                block = 3.0 * sq32[j, e, a] - 2.0 * (block * kept(j, a, e))
                osend[j, a, e] = block.astype(BF)
        if j:
            to = (None, xi, x2, xo)[j]
            outs.append(send(osend.at[j], orecv.at[beta, pl.ds(rows, 2)], to))
    out_ref[beta, pl.ds(rows, 2)] = osend[0]
    for copy, bb, rr in zip(outs, (1 - beta, beta, 1 - beta), (rows, rows_flip, rows_flip)):
        copy.wait_recv()
        out_ref[bb, pl.ds(rr, 2)] = orecv[bb, pl.ds(rr, 2)]
    for copy in started:
        copy.wait_send()


def local(x_blocks, present):
    block = jax.ShapeDtypeStruct
    x = x_blocks.reshape(6, 4, 3, 128, 128)
    purified = pl.pallas_call(
        kernel,
        out_shape=block((2, 4, 3, 128, 128), BF),
        in_specs=[pl.BlockSpec(memory_space=pltpu.VMEM), pl.BlockSpec(memory_space=pltpu.SMEM)],
        out_specs=pl.BlockSpec(memory_space=pltpu.VMEM),
        scratch_shapes=[
            pltpu.VMEM((18, 4, 128, 128), BF),
            pltpu.VMEM((6, 16, 128), F32),
            pltpu.VMEM((3, 16, 128), F32),
            pltpu.VMEM((16, 3, 2, 128, 128), BF),
            pltpu.VMEM((16, 3, 2, 128, 128), BF),
            pltpu.VMEM((4, 4, 7, 4, 128, 128), BF),
            pltpu.VMEM((4, 3, 2, 128, 128), F32),
            pltpu.VMEM((256, 256), F32),
            pltpu.VMEM((256, 256), F32),
            pltpu.VMEM((256, 128), F32),
            pltpu.VMEM((3, 2, 256, 256), F32),
            pltpu.VMEM((4, 2, 3, 128, 128), BF),
            pltpu.VMEM((2, 4, 3, 128, 128), BF),
            pltpu.SemaphoreType.DMA((N_SEMS,)),
            pltpu.SemaphoreType.DMA((N_SEMS,)),
            pltpu.SemaphoreType.DMA((2,)),
        ],
        compiler_params=pltpu.CompilerParams(
            collective_id=0, has_side_effects=True, vmem_limit_bytes=56 * 2**20
        ),
        cost_estimate=pl.CostEstimate(flops=7_500_000_000, bytes_accessed=4_000_000, transcendentals=0),
    )(x, present.reshape(72))
    return purified.astype(F32).reshape(2, 4, 3, 1, 128, 128)


def solution(mesh):
    return jax.shard_map(
        local,
        mesh=mesh,
        in_specs=(P(None, "row", None, "col", None, None), P(None, "row", None, "col")),
        out_specs=P("layer", "row", None, "col", None, None),
        check_vma=False,
    )
```

time: 853 us -> 100 us (0.12)
  waiting for transfers between devices: 644 us -> 0 us
  Pallas kernels: 0 us -> 95.2 us
  starting transfers between devices: 86.7 us -> 0 us
  local copies, waits for them, and re-layouts: 48.5 us -> 1.41 us
  other arithmetic: 29.9 us -> 2.45 us
  matrix products: 27.2 us -> 0 us
  between operations: 13.9 us -> 0.01 us
    ppermute x16 -> x0, waiting for transfers between devices: 433 us -> none  [shifted_2(): lax.ppermute(array, axis, [(i, (i + by) % length) for i in range(length)])]
    pallas_call x0 -> x1, Pallas kernels: none -> 95.2 us  [local(): pl.pallas_call(kernel, out_shape=block((2, 4, 3, 128, 128), BF), in_specs...]
    unnamed x4 -> x0, waiting for transfers between devices: 92.9 us -> none
    psum x1 -> x0, waiting for transfers between devices: 92 us -> none  [local(): square = lax.psum(product(masked[1:region_count + 1]), 'layer') * kept_rows]
    ppermute x16 -> x0, starting transfers between devices: 86.6 us -> none  [shifted_2(): lax.ppermute(array, axis, [(i, (i + by) % length) for i in range(length)])]
    dot_general x48 -> x0, matrix products: 27.2 us -> none  [contract(): jnp.einsum('brdcxy,bdcwyz->brwxz', left_stack, right_stack, preferred_ele...]
    all_gather x1 -> x0, waiting for transfers between devices: 26.9 us -> none  [local(): panel_all = lax.all_gather(masked, 'row', axis=1, tiled=True)]
    slice x17 -> x0, local copies, waits for them, and re-layouts: 21.8 us -> none  [the longest x15 20.5 us: contract(): right_blocks[d_index:d_index + region_count, :, e_index - d_index + 1]]
  transfers between devices with their start and end apart: 19 -> 0, of which waited for: 19 -> 0; matrix products, arithmetic and copies ran while one was open for 7% -> 0% of each run, Pallas kernels for 0% -> 0%
where the time goes in v2:
time: 100 us; the launch traced here: 99.1 us
  Pallas kernels  95.2 us (95%)
  other arithmetic  2.45 us (2%)
  local copies, waits for them, and re-layouts  1.41 us (1%)
    pallas_call x1, Pallas kernels, local(): pl.pallas_call(kernel, out_shape=block((2, 4, 3, 128, 128), BF), in_specs...  95.2 us
    reshape x1, other arithmetic, local(): return purified.astype(F32).reshape(2, 4, 3, 1, 128, 128)  2.45 us

profile of v2, /device:TPU:0, one launch (start us, length us, event | category | flops | bytes accessed | tf_op | source)
XLA Modules:
  0.0 99.1 jit_solution(2689829492931555002)
XLA Ops:
  0.0 0.8 copy.5
  0.8 0.6 reshape.13.pres_ref
  1.4 95.2 %shard_map.28 = bf16[2,4,3,128,128]{4,3,2,1,0:T(8,128)(2,1)} custom-call(bf16[6,4,3,128,128]{4,3,2,1,0:T(8,128)(2,1)} %bitcast.9, s32[72]{0:T(128)} %reshape.13.pres_ref), custom_call_target="tpu_custom_call" | custom-call | flops 7500000256 | bytes 4000000 | tf_op jit(solution)/shard_map/pallas_call | solution.py:294
  96.7 2.5 %bitcast_convert_fusion = f32[2,4,3,1,128,128]{5,4,3,2,1,0:T(8,128)} fusion(bf16[2,4,3,128,128]{4,3,2,1,0:T(8,128)(2,1)} %shard_map.28), kind=kLoop, calls=%fused_computation | loop fusion | flops 393216 | bytes 2359296 | tf_op jit(solution)/shard_map/reshape | solution.py:322

commit v3 on v2

v3 whole, which is shorter than its diff:
```python
import jax
import jax.numpy as jnp
from jax import lax
from jax.experimental import pallas as pl
from jax.experimental.pallas import tpu as pltpu
from jax.sharding import PartitionSpec as P

MESH = pl.DeviceIdType.MESH
BF, F32 = jnp.bfloat16, jnp.float32
N_SEMS = 112
C0, C1, C2, C3 = 0, 1, 2, 3


def kernel(
    x_hbm, pres_ref, out_ref,
    x_ref, xr, pmask, pmask_in, left, sq, right, sq32, acc_a, acc_b, acc_c, cube, osend,
    send_sems, recv_sems, local_sems,
):
    row, col, zl = lax.axis_index("row"), lax.axis_index("col"), lax.axis_index("layer")
    zh, co = row // 2, row % 2
    y, x = col // 4, col % 4
    z = 2 * zh + zl

    def flip1(v):
        return v + 1 - 2 * (v % 2)

    def flip2(v):
        return (v + 2) % 4

    def flip3(v):
        return 3 - v

    def device(z_, y_, x_, co_):
        return (2 * (z_ // 2) + co_, 4 * y_ + x_, z_ % 2)

    columns = (x, flip1(x), flip2(x), flip3(x))
    y1c, y2c, y3c = flip1(y), flip2(y), flip3(y)
    xi, x2, xo = (device(z, y, c, co) for c in columns[1:])
    y1 = device(z, y1c, x, co)
    y3 = device(z, y3c, x, co)
    zo = device(flip3(z), y, x, co)
    z2 = device(flip2(z), y, x, co)
    sib = device(z, y, x, 1 - co)
    partners = (xi, x2, xo, y1, y3, zo, z2, sib)

    x_in = pltpu.make_async_copy(x_hbm, x_ref, local_sems.at[2])
    x_in.start()
    barrier = pltpu.get_barrier_semaphore()
    for partner in partners:
        pl.semaphore_signal(barrier, inc=1, device_id=partner, device_id_type=MESH)

    beta, rho = x // 2, x % 2
    b = 2 * zl + beta
    b_xo = 2 * zl + 1 - beta
    b_zo = 2 * (1 - zl) + beta
    rows = 2 * rho
    rows_flip = 2 - rows
    kg0 = row
    kg1 = 2 * (1 - zh) + co
    m_at, e_at = 3 * (1 - beta), 4 * beta
    m_xo, e_xo = 3 * beta, 4 * (1 - beta)

    def mask_region(q, carry):
        for a in range(4):
            for o in range(3):
                keep = pres_ref[a, o, 0, q].astype(F32)
                xr[3 * q + o, a] = (x_ref[q, a, o].astype(F32) * keep).astype(BF)
                pmask[q, a * 3 + o] = jnp.full((128,), 1.0, F32) * keep
        for i in range(12, 16):
            pmask[q, i] = jnp.zeros((128,), F32)
        return carry

    x_in.wait()
    lax.fori_loop(0, 6, mask_region, 0)
    pl.semaphore_wait(barrier, len(partners))

    started = []

    def send(src, dst, to):
        i = len(started)
        copy = pltpu.make_async_remote_copy(
            src_ref=src, dst_ref=dst, send_sem=send_sems.at[i], recv_sem=recv_sems.at[i],
            device_id=to, device_id_type=MESH,
        )
        copy.start()
        started.append(copy)
        return copy

    def same(ref, to):
        return send(ref, ref, to)

    class Ring:
        def __init__(self, buf, c, wide=1, rows_at=0, count=2):
            self.buf, self.c, self.wide, self.rows = buf, c, wide, pl.ds(rows_at, count)
            self.y1, self.y3 = same(self.at(y), y1), same(self.at(y), y3)

        def at(self, yy, *half):
            return self.buf.at[(pl.ds(4 * yy + self.c, self.wide), slice(None), self.rows, *half)]

        def relay(self):
            self.y1.wait_recv()
            self.a = same(self.at(y1c, pl.ds(0, 64)), y3)
            self.y3.wait_recv()
            self.b = same(self.at(y3c, pl.ds(64, 64)), y1)

        def wait(self):
            self.a.wait_recv()
            self.b.wait_recv()

    def left_of(region, first_row):
        return xr.at[pl.ds(3 * region + 3, 3), pl.ds(first_row, 2)]

    my_left = left.at[4 * y + x]
    own_left_src = left_of(b, rows)
    lp1 = send(left_of(b, rows_flip), my_left, xi)
    lp3 = send(left_of(b_xo, rows_flip), my_left, xo)
    lp2 = send(left_of(b_xo, rows), my_left, x2)
    own_left = pltpu.make_async_copy(own_left_src, my_left, local_sems.at[0])
    own_left.start()

    def native(region, at, size):
        return xr.at[pl.ds(3 * region + 1 + at, size)]

    def panel(j, kg, at=None, size=7):
        return right.at[j, kg] if at is None else right.at[j, kg, pl.ds(at, size)]

    masks = [send(pmask.at[bb + 1], pmask_in.at[i], to) for i, (bb, to) in enumerate(((b, xi), (b_xo, x2), (b_xo, xo)))]
    b_m = send(native(b_zo, m_at, 4), panel(C0, kg0, m_at, 4), zo)
    c_e = send(native(b_xo, e_xo, 3), panel(C3, kg0, e_xo, 3), xo)
    a_m = send(native(b, m_at, 4), panel(C1, kg0, m_at, 4), xi)
    b_e = send(native(b_zo, e_at, 3), panel(C0, kg0, e_at, 3), zo)
    own_right = pltpu.make_async_copy(native(b, 0, 7), panel(C0, kg0), local_sems.at[1])
    own_right.start()
    own_left.wait()
    lp1.wait_recv()
    l_near = Ring(left, 2 * (x // 2), 2)
    a_e = send(native(b, e_at, 3), panel(C1, kg0, e_at, 3), xi)
    sib_0 = send(native(b, 0, 7), panel(C0, kg0), sib)
    lp3.wait_recv()
    lp2.wait_recv()
    l_far = Ring(left, 2 * (1 - x // 2), 2)
    b_m.wait_recv()
    g_m = send(panel(C0, kg1, m_at, 4), panel(C3, kg1, m_xo, 4), xo)
    sib_b_m = same(panel(C0, kg1, m_at, 4), sib)
    c_e.wait_recv()
    h_e = same(panel(C3, kg0, e_at, 3), z2)
    e_e = send(panel(C3, kg0, e_at, 3), panel(C2, kg0, e_at, 3), xi)
    c_m = send(native(b_xo, m_xo, 4), panel(C3, kg0, m_xo, 4), xo)
    sib_c_e = same(panel(C3, kg0, e_at, 3), sib)
    l_near.relay()
    b_e.wait_recv()
    sib_b_e = same(panel(C0, kg1, e_at, 3), sib)
    a_m.wait_recv()
    f_m = send(panel(C1, kg0, m_at, 4), panel(C2, kg0, m_xo, 4), xo)
    sib_a_m = same(panel(C1, kg0, m_at, 4), sib)
    l_far.relay()
    a_e.wait_recv()
    d_m = same(panel(C1, kg0, m_at, 4), z2)
    d_e = same(panel(C1, kg0, e_at, 3), z2)
    sib_a_e = same(panel(C1, kg0, e_at, 3), sib)
    g_m.wait_recv()
    i_m = send(panel(C3, kg1, m_at, 4), panel(C2, kg1, m_at, 4), xi)
    sib_g = same(panel(C3, kg1, m_at, 4), sib)

    def part(j, kg, half):
        return right.at[j, kg, pl.ds(e_at, 3), pl.ds(2 * half, 2)]

    def square_half(j, first):
        def lhs(kg, d):
            return jnp.concatenate([left[4 * kg + k, d].reshape(256, 128) for k in range(4)], axis=1)

        def block(kg, g):
            return right[j, kg, g].reshape(512, 128)

        if first:
            acc_a[...] = jnp.zeros_like(acc_a)
            acc_b[...] = jnp.zeros_like(acc_b)
            acc_c[...] = jnp.zeros_like(acc_c)
        start = 2 * zh if first else 2 * (1 - zh)

        def group(i, carry):
            kg = start + i
            l_0, l_1, l_2 = lhs(kg, 0), lhs(kg, 1), lhs(kg, 2)
            r = [block(kg, g) for g in range(7)]
            acc_a[...] += jnp.dot(
                jnp.concatenate([l_0, l_1], axis=1),
                jnp.concatenate(
                    [jnp.concatenate([r[0], r[1]], axis=1), jnp.concatenate([r[2], r[3]], axis=1)], axis=0
                ),
                preferred_element_type=F32,
            )
            acc_b[...] += jnp.dot(l_2, jnp.concatenate([r[5], r[6]], axis=1), preferred_element_type=F32)
            acc_c[...] += jnp.dot(l_1, r[4], preferred_element_type=F32)
            return carry

        lax.fori_loop(0, 2, group, 0)

    def kept(j, a, e):
        i = (rows + a) * 3 + e
        return pmask[b + 1, pl.ds(i, 1)] if j == 0 else pmask_in[j - 1, pl.ds(i, 1)]

    def square_store(j, a):
        at = slice(a * 128, a * 128 + 128)
        out = (
            acc_a[at, :128],
            acc_a[at, 128:] + acc_b[at, :128],
            acc_b[at, 128:] + acc_c[at],
        )
        for e in range(3):
            block = out[e] * kept(j, a, e)
            sq32[j, e, a] = block
            sq[4 * y + columns[j], e, a] = block.astype(BF)

    def square_column(j):
        square_half(j, True)
        square_half(j, False)
        square_store(j, 0)
        square_store(j, 1)
        return Ring(sq, columns[j])

    def cube_part(j, first=False, row_at=0, count=2, halves=(0, 1)):
        c, m = columns[j], 128 * count
        at = slice(row_at * 128, row_at * 128 + m)
        for e in range(3):
            offsets = [d for d in range(3) if 0 <= e - d + 1 <= 2]
            lhs = jnp.concatenate(
                [
                    sq[4 * yy + c, d, row_at : row_at + count].reshape(m, 128)
                    for d in offsets for yy in range(4)
                ],
                axis=1,
            )
            for half in halves:
                rhs = jnp.concatenate(
                    [
                        jnp.concatenate([right[2 * half + i, yy, 2 * d + e, c] for i in range(2)], axis=1)
                        for d in offsets for yy in range(4)
                    ],
                    axis=0,
                )
                part = jnp.dot(lhs, rhs, preferred_element_type=F32)
                if first:
                    cube[e, half, at] = part
                else:
                    cube[e, half, at] += part

    outs = []

    def result_row(a):
        for j in (2, 1, 3, 0):
            for e in range(3):
                block = cube[e, j // 2, a * 128 : a * 128 + 128, (j % 2) * 128 : (j % 2) * 128 + 128]
                block = (3.0 * sq32[j, e, a] - 2.0 * (block * kept(j, a, e))).astype(BF)
                if j:
                    osend[j, a, e] = block
                else:
                    out_ref[beta, rows + a, e] = block
            if j:
                outs.append(send(osend.at[j, a], out_ref.at[beta, rows + a], (None, xi, x2, xo)[j]))

    def arrived(*copies):
        for copy in copies:
            copy.wait_recv()

    arrived(*masks)
    l_near.wait()
    l_far.wait()
    own_right.wait()
    arrived(sib_0, sib_b_m, sib_b_e)
    s0 = square_column(C0)
    e_e.wait_recv()
    j_e = same(part(C2, kg0, 1), z2)
    sib_e = same(panel(C2, kg0, e_at, 3), sib)
    h_e.wait_recv()
    i_e = send(part(C3, kg1, 0), part(C2, kg1, 0), xi)
    sib_h = same(panel(C3, kg1, e_at, 3), sib)
    c_m.wait_recv()
    sib_c_m = same(panel(C3, kg0, m_at, 4), sib)
    s0.relay()
    arrived(sib_g, sib_h, sib_c_e, sib_c_m)
    s3 = square_column(C3)
    arrived(sib_a_m, sib_a_e)
    square_half(C1, True)
    i_m.wait_recv()
    sib_i_m = same(panel(C2, kg1, m_at, 4), sib)
    d_m.wait_recv()
    sib_d_m = same(panel(C1, kg1, m_at, 4), sib)
    s3.relay()
    d_e.wait_recv()
    sib_d_e = same(panel(C1, kg1, e_at, 3), sib)
    f_m.wait_recv()
    sib_f = same(panel(C2, kg0, m_at, 4), sib)
    arrived(sib_d_m, sib_d_e)
    square_half(C1, False)
    square_store(C1, 0)
    s1 = [Ring(sq, columns[C1], 1, 0, 1)]
    square_store(C1, 1)
    i_e.wait_recv()
    sib_i_e = same(part(C2, kg1, 0), sib)
    j_e.wait_recv()
    sib_j_e = same(part(C2, kg1, 1), sib)
    arrived(sib_f, sib_e)
    square_half(C2, True)
    arrived(sib_i_m, sib_i_e, sib_j_e)
    square_half(C2, False)
    square_store(C2, 0)
    s2 = [Ring(sq, columns[C2], 1, 0, 1)]
    square_store(C2, 1)
    s1[0].relay()
    s0.wait()
    cube_part(C0, True, halves=(0,))
    s2[0].relay()
    s1.append(Ring(sq, columns[C1], 1, 1, 1))
    s2.append(Ring(sq, columns[C2], 1, 1, 1))
    cube_part(C0, True, halves=(1,))
    s3.wait()
    cube_part(C3)
    s1[0].wait()
    cube_part(C1, False, 0, 1)
    s2[0].wait()
    cube_part(C2, False, 0, 1)
    s1[1].relay()
    s2[1].relay()
    result_row(0)
    s1[1].wait()
    cube_part(C1, False, 1, 1)
    s2[1].wait()
    cube_part(C2, False, 1, 1)
    result_row(1)
    arrived(*outs)
    for copy in started:
        copy.wait_send()


def local(x_blocks, present):
    block = jax.ShapeDtypeStruct
    x = x_blocks.reshape(6, 4, 3, 128, 128)
    purified = pl.pallas_call(
        kernel,
        out_shape=block((2, 4, 3, 128, 128), BF),
        in_specs=[pl.BlockSpec(memory_space=pl.ANY), pl.BlockSpec(memory_space=pltpu.SMEM)],
        out_specs=pl.BlockSpec(memory_space=pltpu.VMEM),
        scratch_shapes=[
            pltpu.VMEM((6, 4, 3, 128, 128), BF),
            pltpu.VMEM((18, 4, 128, 128), BF),
            pltpu.VMEM((6, 16, 128), F32),
            pltpu.VMEM((3, 16, 128), F32),
            pltpu.VMEM((16, 3, 2, 128, 128), BF),
            pltpu.VMEM((16, 3, 2, 128, 128), BF),
            pltpu.VMEM((4, 4, 7, 4, 128, 128), BF),
            pltpu.VMEM((4, 3, 2, 128, 128), F32),
            pltpu.VMEM((256, 256), F32),
            pltpu.VMEM((256, 256), F32),
            pltpu.VMEM((256, 128), F32),
            pltpu.VMEM((3, 2, 256, 256), F32),
            pltpu.VMEM((4, 2, 3, 128, 128), BF),
            pltpu.SemaphoreType.DMA((N_SEMS,)),
            pltpu.SemaphoreType.DMA((N_SEMS,)),
            pltpu.SemaphoreType.DMA((3,)),
        ],
        compiler_params=pltpu.CompilerParams(
            collective_id=0, has_side_effects=True, vmem_limit_bytes=44 * 2**20
        ),
        cost_estimate=pl.CostEstimate(flops=7_500_000_000, bytes_accessed=4_000_000, transcendentals=0),
    )(
        pltpu.with_memory_space_constraint(x, pltpu.HBM),
        pltpu.with_memory_space_constraint(present.transpose(1, 2, 3, 0), pltpu.HBM),
    )
    return purified.astype(F32).reshape(2, 4, 3, 1, 128, 128)


def solution(mesh):
    return jax.shard_map(
        local,
        mesh=mesh,
        in_specs=(P(None, "row", None, "col", None, None), P(None, "row", None, "col")),
        out_specs=P("layer", "row", None, "col", None, None),
        check_vma=False,
    )
```

time: 100 us -> 90.9 us (0.909)
  Pallas kernels: 95.2 us -> 89.4 us
  local copies, waits for them, and re-layouts: 1.41 us -> 0 us
  other arithmetic: 2.45 us -> 1.32 us
    pallas_call x1, Pallas kernels: 95.2 us -> 89.4 us  [local(): pl.pallas_call(kernel, out_shape=block((2, 4, 3, 128, 128), BF), in_specs...]
    reshape x1, other arithmetic: 2.45 us -> 1.32 us  [local(): return purified.astype(F32).reshape(2, 4, 3, 1, 128, 128)]
where the time goes in v3:
time: 90.9 us; the launch traced here: 90.7 us
  Pallas kernels  89.4 us (98%)
  other arithmetic  1.32 us (1%)
    pallas_call x1, Pallas kernels, local(): pl.pallas_call(kernel, out_shape=block((2, 4, 3, 128, 128), BF), in_specs...  89.4 us

profile of v3, /device:TPU:0, one launch (start us, length us, event | category | flops | bytes accessed | tf_op | source)
XLA Modules:
  0.0 90.7 jit_solution(11751789075149385719)
XLA Ops:
  0.0 89.4 %shard_map.28 = bf16[2,4,3,128,128]{4,3,2,1,0:T(8,128)(2,1)S(1)} custom-call(bf16[6,4,3,128,128]{4,3,2,1,0:T(8,128)(2,1)} %bitcast.8, s32[4,3,1,6]{3,2,1,0:T(1,128)} %bitcast.9), custom_call_target="tpu_custom_call" | custom-call | flops 7500000256 | bytes 4000000 | tf_op jit(solution)/shard_map/pallas_call | solution.py:338
  89.4 1.3 %bitcast_convert_fusion = f32[2,4,3,1,128,128]{5,4,3,2,1,0:T(8,128)} fusion(bf16[2,4,3,128,128]{4,3,2,1,0:T(8,128)(2,1)S(1)} %shard_map.28), kind=kLoop, calls=%fused_computation | loop fusion | flops 393216 | bytes 2359296 | tf_op jit(solution)/shard_map/reshape | solution.py:369

commit v4 on v3

--- a/solution.py
+++ b/solution.py
@@ -9,6 +9,7 @@
 BF, F32 = jnp.bfloat16, jnp.float32
 N_SEMS = 112
 C0, C1, C2, C3 = 0, 1, 2, 3
+PAIRS = ((C0, C3), (C1, C2))
 
 
 def kernel(
@@ -218,7 +219,7 @@
         square_store(j, 1)
         return Ring(sq, columns[j])
 
-    def cube_part(j, first=False, row_at=0, count=2, halves=(0, 1)):
+    def cube_part(j, first=False, row_at=0, count=2, halves=(0, 1), ys=(0, 1, 2, 3)):
         c, m = columns[j], 128 * count
         at = slice(row_at * 128, row_at * 128 + m)
         for e in range(3):
@@ -226,15 +227,15 @@
             lhs = jnp.concatenate(
                 [
                     sq[4 * yy + c, d, row_at : row_at + count].reshape(m, 128)
-                    for d in offsets for yy in range(4)
+                    for d in offsets for yy in ys
                 ],
                 axis=1,
             )
             for half in halves:
                 rhs = jnp.concatenate(
                     [
-                        jnp.concatenate([right[2 * half + i, yy, 2 * d + e, c] for i in range(2)], axis=1)
-                        for d in offsets for yy in range(4)
+                        jnp.concatenate([right[j, yy, 2 * d + e, c] for j in PAIRS[half]], axis=1)
+                        for d in offsets for yy in ys
                     ],
                     axis=0,
                 )
@@ -247,9 +248,11 @@
     outs = []
 
     def result_row(a):
-        for j in (2, 1, 3, 0):
+        for j in (C2, C1, C3, C0):
+            half = 0 if j in PAIRS[0] else 1
+            at = PAIRS[half].index(j)
             for e in range(3):
-                block = cube[e, j // 2, a * 128 : a * 128 + 128, (j % 2) * 128 : (j % 2) * 128 + 128]
+                block = cube[e, half, a * 128 : a * 128 + 128, at * 128 : at * 128 + 128]
                 block = (3.0 * sq32[j, e, a] - 2.0 * (block * kept(j, a, e))).astype(BF)
                 if j:
                     osend[j, a, e] = block
@@ -281,6 +284,8 @@
     s3 = square_column(C3)
     arrived(sib_a_m, sib_a_e)
     square_half(C1, True)
+    s0.wait()
+    cube_part(C0, True, halves=(0,))
     i_m.wait_recv()
     sib_i_m = same(panel(C2, kg1, m_at, 4), sib)
     d_m.wait_recv()
@@ -288,12 +293,12 @@
     s3.relay()
     d_e.wait_recv()
     sib_d_e = same(panel(C1, kg1, e_at, 3), sib)
-    f_m.wait_recv()
-    sib_f = same(panel(C2, kg0, m_at, 4), sib)
     arrived(sib_d_m, sib_d_e)
     square_half(C1, False)
     square_store(C1, 0)
     s1 = [Ring(sq, columns[C1], 1, 0, 1)]
+    f_m.wait_recv()
+    sib_f = same(panel(C2, kg0, m_at, 4), sib)
     square_store(C1, 1)
     i_e.wait_recv()
     sib_i_e = same(part(C2, kg1, 0), sib)
@@ -307,29 +312,31 @@
     s2 = [Ring(sq, columns[C2], 1, 0, 1)]
     square_store(C2, 1)
     s1[0].relay()
-    s0.wait()
-    cube_part(C0, True, halves=(0,))
+    cube_part(C0, True, halves=(1,))
+    s3.wait()
     s2[0].relay()
     s1.append(Ring(sq, columns[C1], 1, 1, 1))
     s2.append(Ring(sq, columns[C2], 1, 1, 1))
-    cube_part(C0, True, halves=(1,))
-    s3.wait()
     cube_part(C3)
     s1[0].wait()
     cube_part(C1, False, 0, 1)
+    cube_part(C2, False, 0, 1, ys=(y, y1c, y3c))
     s2[0].wait()
-    cube_part(C2, False, 0, 1)
+    cube_part(C2, False, 0, 1, ys=(y2c,))
+    result_row(0)
     s1[1].relay()
     s2[1].relay()
-    result_row(0)
+    cube_part(C2, False, 1, 1, ys=(y, y1c, y3c))
     s1[1].wait()
     cube_part(C1, False, 1, 1)
     s2[1].wait()
-    cube_part(C2, False, 1, 1)
+    cube_part(C2, False, 1, 1, ys=(y2c,))
     result_row(1)
-    arrived(*outs)
     for copy in started:
-        copy.wait_send()
+        if all(copy is not other for other in outs):
+            copy.wait_send()
+    for copy in outs:
+        copy.wait()
 
 
 def local(x_blocks, present):

time: 90.9 us -> 90.1 us (level)
  no operation moved by 1% of the time
where the time goes in v4:
time: 90.1 us; the launch traced here: 89.9 us
  Pallas kernels  88.6 us (98%)
  other arithmetic  1.32 us (1%)
    pallas_call x1, Pallas kernels, local(): pl.pallas_call(kernel, out_shape=block((2, 4, 3, 128, 128), BF), in_specs...  88.6 us

profile of v4, /device:TPU:0, one launch (start us, length us, event | category | flops | bytes accessed | tf_op | source)
XLA Modules:
  0.0 89.9 jit_solution(7463318496166370520)
XLA Ops:
  0.0 88.6 %shard_map.28 = bf16[2,4,3,128,128]{4,3,2,1,0:T(8,128)(2,1)S(1)} custom-call(bf16[6,4,3,128,128]{4,3,2,1,0:T(8,128)(2,1)} %bitcast.8, s32[4,3,1,6]{3,2,1,0:T(1,128)} %bitcast.9), custom_call_target="tpu_custom_call" | custom-call | flops 7500000256 | bytes 4000000 | tf_op jit(solution)/shard_map/pallas_call | solution.py:345
  88.6 1.3 %bitcast_convert_fusion = f32[2,4,3,1,128,128]{5,4,3,2,1,0:T(8,128)} fusion(bf16[2,4,3,128,128]{4,3,2,1,0:T(8,128)(2,1)S(1)} %shard_map.28), kind=kLoop, calls=%fused_computation | loop fusion | flops 393216 | bytes 2359296 | tf_op jit(solution)/shard_map/reshape | solution.py:376

commit v5 on v4

--- a/solution.py
+++ b/solution.py
@@ -164,7 +164,7 @@
     sib_g = same(panel(C3, kg1, m_at, 4), sib)
 
     def part(j, kg, half):
-        return right.at[j, kg, pl.ds(e_at, 3), pl.ds(2 * half, 2)]
+        return right.at[j, kg, pl.ds(e_at, 3), pl.ds(half, 1 + 2 * half)]
 
     def square_half(j, first):
         def lhs(kg, d):

time: 90.1 us -> 92.5 us (1.027)
  Pallas kernels: 88.6 us -> 91 us
    pallas_call x1, Pallas kernels: 88.6 us -> 91 us  [local(): pl.pallas_call(kernel, out_shape=block((2, 4, 3, 128, 128), BF), in_specs...]
where the time goes in v5:
time: 92.5 us; the launch traced here: 92.3 us
  Pallas kernels  91 us (98%)
  other arithmetic  1.32 us (1%)
    pallas_call x1, Pallas kernels, local(): pl.pallas_call(kernel, out_shape=block((2, 4, 3, 128, 128), BF), in_specs...  91 us

profile of v5, /device:TPU:0, one launch (start us, length us, event | category | flops | bytes accessed | tf_op | source)
XLA Modules:
  0.0 92.3 jit_solution(5524327055861431124)
XLA Ops:
  0.0 91.0 %shard_map.28 = bf16[2,4,3,128,128]{4,3,2,1,0:T(8,128)(2,1)S(1)} custom-call(bf16[6,4,3,128,128]{4,3,2,1,0:T(8,128)(2,1)} %bitcast.8, s32[4,3,1,6]{3,2,1,0:T(1,128)} %bitcast.9), custom_call_target="tpu_custom_call" | custom-call | flops 7500000256 | bytes 4000000 | tf_op jit(solution)/shard_map/pallas_call | solution.py:345
  91.0 1.3 %bitcast_convert_fusion = f32[2,4,3,1,128,128]{5,4,3,2,1,0:T(8,128)} fusion(bf16[2,4,3,128,128]{4,3,2,1,0:T(8,128)(2,1)S(1)} %shard_map.28), kind=kLoop, calls=%fused_computation | loop fusion | flops 393216 | bytes 2359296 | tf_op jit(solution)/shard_map/reshape | solution.py:376
